TPU v7x, 32 devices: a whole 2x2x4 slice. The times are simulated.
32 devices in a mesh: tiles: 2 (over y), band: 4 (over x, core), head: 4 (over z).
Axes of the slice: x: 2, y: 2, z: 4, core: 2. Of those that a mesh axis runs over, the one named last changes fastest.
Arguments:
- tokens: bfloat16 [8192, 1024], P(('tiles', 'band')), parts along dimension 0, may hold values from -24 to 24
- w_query: bfloat16 [1024, 1024], P(None, 'head'), may hold values from -0.375 to 0.375
- w_key: bfloat16 [1024, 1024], P(None, 'head'), may hold values from -0.1875 to 0.1875
- w_value: bfloat16 [1024, 1024], P(None, 'head'), may hold values from -0.1875 to 0.1875
- w_out: bfloat16 [1024, 1024], P('head'), may hold values from -0.75 to 0.75
- block_mask: int32 [64, 32], P('tiles'), parts along dimension 0, may hold values from 0 to 1, as said below
Outputs:
- projected: bfloat16 [8192, 1024], P(('tiles', 'band', 'head')), parts along dimension 0
There are 2 independent parts, one for each index of `tiles`. A program takes and returns all parts, laid end to end along the dimension named above; an argument that names none is the same for every part. Nothing has to cross between parts.
Inputs may be any that keep to these rules, and one draw needn't show every extreme that they name: `block_mask`: entries are 0 or 1. Every query block may attend to at least one key block. Among the 8 key blocks of one band at most 6 are named by some query block, and some band has exactly 6.
All inputs are finite; a program needn't handle non-finite values.
Results may differ from a plain program's by a relative error of at most 0.02.
Values may be sent and summed in bfloat16 or wider, within the bound.
A program may use at most 128 MiB of HBM per device.

v0:
```python
import jax
import jax.numpy as jnp
from jax import lax
from jax.sharding import PartitionSpec as P

HD = 64
BLK = 128


rows_per_turn = 8192
neg_large = -1e30


def attend(item_rows, item_block, block_mask, kv_table, kv_where, head_count):
    item_count, item_len, local_cols = item_rows.shape
    key_blocks = block_mask.shape[1]
    head_dim = local_cols // head_count
    score_scale = head_dim ** (-0.5)
    allowed = jnp.take(block_mask, item_block, axis=0).reshape(-1)
    pair_total = item_count * key_blocks
    pair_order = jnp.argsort((1 - allowed) * pair_total + jnp.arange(pair_total, dtype=jnp.int32))
    pair_count = jnp.sum(allowed)
    per_turn = max(1, rows_per_turn // item_len)
    padded_len = -(-pair_total // per_turn) * per_turn
    pair_order = jnp.concatenate([pair_order, jnp.zeros((padded_len - pair_total,), jnp.int32)])
    turn_count = (pair_count + per_turn - 1) // per_turn
    slot_ids = jnp.arange(per_turn, dtype=jnp.int32)
    table_rows = kv_table.shape[0]

    def one_turn(turn_index, carried):
        run_peak, run_mass, run_sum = carried
        chosen = lax.dynamic_slice_in_dim(pair_order, turn_index * per_turn, per_turn)
        is_live = turn_index * per_turn + slot_ids < pair_count
        owners = chosen // key_blocks
        key_block = chosen % key_blocks
        query_rows = jnp.take(item_rows, owners, axis=0).reshape(
            per_turn, item_len, head_count, head_dim
        )
        table_pos = jnp.clip(jnp.take(kv_where, key_block), 0, table_rows - 1)
        pair_rows = jnp.take(kv_table, table_pos, axis=0)
        key_rows = pair_rows[:, :, :local_cols].reshape(per_turn, -1, head_count, head_dim)
        value_rows = pair_rows[:, :, local_cols:].reshape(per_turn, -1, head_count, head_dim)
        scores = (
            jnp.einsum("prhd,pkhd->prhk", query_rows, key_rows, preferred_element_type=jnp.float32)
            * score_scale
        )
        row_peak = jnp.max(scores, axis=3)
        exponent = jnp.exp(scores - row_peak[..., None])
        row_mass = jnp.sum(exponent, axis=3)
        weights = exponent.astype(jnp.bfloat16)
        partial_out = jnp.einsum(
            "prhk,pkhd->prhd", weights, value_rows, preferred_element_type=jnp.float32
        )
        live_peak = jnp.where(is_live[:, None, None], row_peak, neg_large)
        turn_peak = jax.ops.segment_max(live_peak, owners, num_segments=item_count)
        new_peak = jnp.maximum(run_peak, turn_peak)
        factor = jnp.exp(run_peak - new_peak)
        pair_scale = jnp.where(
            is_live[:, None, None], jnp.exp(live_peak - jnp.take(new_peak, owners, axis=0)), 0.0
        )
        mass_terms = jnp.where(is_live[:, None, None], row_mass * pair_scale, 0.0)
        sum_terms = jnp.where(
            is_live[:, None, None, None], partial_out * pair_scale[..., None], 0.0
        )
        run_mass = run_mass * factor + jax.ops.segment_sum(
            mass_terms, owners, num_segments=item_count
        )
        run_sum = run_sum * factor[..., None] + jax.ops.segment_sum(
            sum_terms, owners, num_segments=item_count
        )
        return (new_peak, run_mass, run_sum)

    start_state = (
        jnp.full((item_count, item_len, head_count), neg_large, jnp.float32),
        jnp.zeros((item_count, item_len, head_count), jnp.float32),
        jnp.zeros((item_count, item_len, head_count, head_dim), jnp.float32),
    )
    run_peak, run_mass, run_sum = lax.fori_loop(0, turn_count, one_turn, start_state)
    return (
        (run_sum / run_mass[..., None])
        .reshape(item_count, item_len, local_cols)
        .astype(jnp.bfloat16)
    )


def on_device(tokens, w_query, w_key, w_value, w_out, block_mask):
    band_place = lax.axis_index("band")
    tok_rows = tokens.shape[0]
    local_cols = w_query.shape[1]
    head_count = local_cols // HD
    own_blocks = tok_rows // BLK
    key_blocks = block_mask.shape[1]
    queries = jnp.dot(tokens, w_query, preferred_element_type=jnp.float32).astype(jnp.bfloat16)
    key_part = jnp.dot(tokens, w_key, preferred_element_type=jnp.float32).astype(jnp.bfloat16)
    value_part = jnp.dot(tokens, w_value, preferred_element_type=jnp.float32).astype(jnp.bfloat16)
    key_value = jnp.concatenate([key_part, value_part], axis=1)
    kv_table = lax.all_gather(key_value, "band", axis=0, tiled=True).reshape(
        key_blocks, BLK, 2 * local_cols
    )
    kv_where = jnp.arange(key_blocks, dtype=jnp.int32)
    item_rows = queries.reshape(own_blocks, BLK, local_cols)
    item_block = band_place * own_blocks + jnp.arange(own_blocks, dtype=jnp.int32)
    attended = attend(item_rows, item_block, block_mask, kv_table, kv_where, head_count).reshape(
        tok_rows, local_cols
    )
    projected = lax.psum_scatter(
        jnp.dot(attended, w_out, preferred_element_type=jnp.float32).astype(jnp.bfloat16),
        "head",
        scatter_dimension=0,
        tiled=True,
    )
    return projected


def solution(mesh):
    return jax.shard_map(
        on_device,
        mesh=mesh,
        in_specs=(
            P(("tiles", "band"), None),
            P(None, "head"),
            P(None, "head"),
            P(None, "head"),
            P("head", None),
            P("tiles", None),
        ),
        out_specs=P(("tiles", "band", "head"), None),
        check_vma=False,
    )
```

profile of v0, /device:TPU:0, one launch (start us, length us, event | category | flops | bytes accessed | tf_op | source)
XLA Modules:
  0.0 315.1 jit_solution(12742740644684946796)
XLA Ops:
  6.5 0.0 copy-start
  6.5 0.0 copy-start.3
  6.5 0.0 all-gather.2.cloned.1.call-start
  6.5 1.6 copy-done
  8.1 1.8 convolution_convert_fusion.2
  9.9 1.8 convolution_convert_fusion.3
  11.7 1.0 pad_maximum_fusion
  12.8 0.0 all-gather.2.cloned.1.call-update
  12.8 0.0 reduce-scatter.2.cloned.1.call-start
  12.9 0.0 copy-done.3
  12.9 0.6 gather_fusion.4
  13.5 0.8 subtract_multiply_fusion
  14.9 0.1 mul.72
  15.0 3.2 %sort.17 = (s32[256]{0:T(256)}, s32[256]{0:T(256)S(1)}) sort(s32[256]{0:T(256)S(1)} %iota_add_fusion.1, s32[256]{0:T(256)S(1)} %iota.22), dimensions={0}, to_apply=%region_1.2 | sort | flops 2048 | bytes 4096 | tf_op jit(solution)/shard_map/jit(argsort)/sort | solution.py:21
  18.2 2.5 convolution_convert_fusion.1
  20.7 0.0 copy-start.2
  20.7 29.4 %all-gather.2.cloned.1.call-done = bf16[4096,512]{0,1:T(8,128)(2,1)} async-done(((bf16[1024,512]{0,1:T(8,128)(2,1)}), bf16[4096,512]{0,1:T(8,128)(2,1)}) %all-gather.2.cloned.1.call-update) | async-done | bytes 4194320 | tf_op jit(solution)/shard_map/all_gather | solution.py:97
  50.1 6.5 %copy.24 = bf16[4096,512]{1,0:T(8,128)(2,1)} copy(bf16[4096,512]{0,1:T(8,128)(2,1)} %all-gather.2.cloned.1.call-done) | data formatting | bytes 8388608
  56.6 0.1 broadcast.242
  56.7 0.0 copy-done.2
  56.8 102.0 %while.17 = (s32[]{:T(128)}, f32[8,128,4]{1,2,0:T(4,128)S(1)}, f32[8,128,4]{1,2,0:T(4,128)S(1)}, f32[8,128,4,64]{1,3,2,0:T(8,128)S(1)}, s32[]{:T(128)}, /*index=...) while((s32[]{:T(128)}, f32[8,128,4]{1,2,0:T(4,128)S(1)}, ...), condition=%wide.region_8.9_spmd.clone, body=%wide.region_2.8_spmd.clone.sunk | while | flops 1120389376 | bytes 185223568 | solution.py:78
  57.0 0.8 compare_and_fusion.5
  57.8 0.8 gather_fusion
  58.6 7.7 %gather_fusion.1 = bf16[64,128,512]{2,1,0:T(8,128)(2,1)} fusion(bf16[32,128,512]{2,1,0:T(8,128)(2,1)} %get-tuple-element.364, s32[1024]{0:T(1024)S(1)} %pad_clamp_fusion.8), kind=kCustom, calls=%fused_computation.1.clone.clone.1 | custom fusion | bytes 16777472 | tf_op jit(solution)/shard_map/while/body/jit(_take)/gather | solution.py:40
  66.3 7.5 %broadcast_select_fusion.4 = bf16[64,128,512]{2,1,0:T(8,128)(2,1)} fusion(bf16[64,128,512]{2,1,0:T(8,128)(2,1)} %gather_fusion.1, pred[64]{0:T(512)(128)(4,1)S(1)} %get-tuple-element.317), kind=kLoop, calls=%fused_computation.20.clone.1 | loop fusion | flops 4194304 | bytes 16777280 | tf_op jit(solution)/shard_map/while/body/jit(_take)/select_n | solution.py:40
  73.8 6.0 %fusion.45 = (bf16[64,128,256]{2,1,0:T(8,128)(2,1)}, bf16[64,128,256]{2,1,0:T(8,128)(2,1)}) fusion(bf16[64,128,512]{2,1,0:T(8,128)(2,1)} %broadcast_select_fusion.4), kind=kLoop, calls=%fused_computation.65.clone.1 | loop fusion | bytes 16777216 | tf_op jit(solution)/shard_map/while/body/slice | solution.py:42
  79.8 6.4 %copy.33 = bf16[64,128,256]{1,2,0:T(8,128)(2,1)} copy(bf16[64,128,256]{2,1,0:T(8,128)(2,1)} %get-tuple-element.318) | data formatting | bytes 8388608 | tf_op jit(solution)/shard_map/while/body/slice | solution.py:41
  86.1 2.7 gather_fusion.2
  88.9 6.4 %copy.34 = bf16[64,128,256]{1,2,0:T(8,128)(2,1)} copy(bf16[64,128,256]{2,1,0:T(8,128)(2,1)} %gather_fusion.2) | data formatting | bytes 8388608 | tf_op jit(solution)/shard_map/while/body/jit(_take)/gather | solution.py:36
  95.3 12.2 %bitcast_reduce_fusion.2 = (f32[64,128,4]{1,2,0:T(4,128)S(1)}, f32[64,4,128,128]{3,2,1,0:T(8,128)}) fusion(bf16[64,128,4,64]{1,3,2,0:T(8,128)(2,1)} %bitcast.83, bf16[64,128,4,64]{1,3,2,0:T(8,128)(2,1)} %bitcast.85, pred[64]{0:T(512)(128)(4,1)S(1)} %get-tuple-element.319), kind=kOutput, calls=%fused_computation.11.clone.1 | convolution fusion | flops 547323904 | bytes 25296960 | tf_op jit(solution)/shard_map/while/body/prhd,pkhd->prhk/dot_general | solution.py:44
  107.5 0.1 broadcast_select_fusion.5
  107.7 2.9 scatter_fusion
  110.6 10.7 %fusion.47 = f32[64,128,4]{1,2,0:T(4,128)S(1)} fusion(f32[64,4,128,128]{3,2,1,0:T(8,128)} %get-tuple-element.325, f32[64,128,4]{1,2,0:T(4,128)S(1)} %get-tuple-element.320), kind=kLoop, calls=%fused_computation.14.clone.1 | loop fusion | flops 12550144 | bytes 17039360 | tf_op jit(solution)/shard_map/while/body/reduce_sum | solution.py:49
  121.3 0.7 gather_fusion.3
  121.9 0.2 multiply_select_fusion.2
  122.2 2.9 scatter_fusion.1
  125.0 0.2 broadcast_multiply_fusion.2
  125.3 6.4 %copy.35 = bf16[64,128,256]{1,2,0:T(8,128)(2,1)} copy(bf16[64,128,256]{2,1,0:T(8,128)(2,1)} %get-tuple-element.328) | data formatting | bytes 8388608 | tf_op jit(solution)/shard_map/while/body/slice | solution.py:42
  131.7 14.6 %fusion.48 = f32[64,128,4,64]{1,3,2,0:T(8,128)} fusion(f32[64,128,4]{1,2,0:T(4,128)S(1)} %get-tuple-element.327, pred[64]{0:T(512)(128)(4,1)S(1)} %get-tuple-element.321, bf16[64,128,4,64]{1,3,2,0:T(8,128)(2,1)} %bitcast.84, f32[64,4,128,128]{3,2,1,0:T(8,128)} %get-tuple-element.325, f32[64,128,4]{1,2,0:T(4,128)S(1)} %get-tuple-element.320), kind=kOutput, calls=%fused_computation.17.clone.1 | convolution fusion | flops 553648128 | bytes 29622336 | tf_op jit(solution)/shard_map/while/body/prhk,pkhd->prhd/dot_general | solution.py:51
  146.2 12.3 %scatter_fusion.2 = f32[8,128,4,64]{1,3,2,0:T(8,128)S(1)} fusion(f32[8,128,4,64]{1,3,2,0:T(8,128)S(1)} %broadcast_multiply_fusion.2, s32[64]{0:T(128)S(1)} %get-tuple-element.314, f32[64,128,4,64]{1,3,2,0:T(8,128)} %fusion.48), kind=kCustom, calls=%fused_computation.7.clone.clone.1 | custom fusion | flops 2097152 | bytes 25166080 | tf_op jit(solution)/shard_map/while/body/scatter-add | solution.py:68
  158.8 0.0 copy-start.1
  158.8 0.1 divide_convert_fusion
  158.9 0.3 copy.22
  159.3 3.3 %convolution_convert_fusion = bf16[1024,1024]{1,0:T(8,128)(2,1)} fusion(bf16[256,1024]{1,0:T(8,128)(2,1)} %param.12, bf16[32,8,8,128]{3,2,1,0:T(8,128)(2,1)S(1)} %bitcast.86), kind=kOutput, calls=%fused_computation.48 | convolution fusion | flops 537919488 | bytes 3145728 | tf_op jit(solution)/shard_map/dot_general | solution.py:107
  162.6 0.0 reduce-scatter.2.cloned.1.call-update
  162.6 145.6 %reduce-scatter.2.cloned.1.call-done = bf16[256,1024]{1,0:T(8,128)(2,1)} async-done(((bf16[1024,1024]{1,0:T(8,128)(2,1)}), bf16[256,1024]{1,0:T(8,128)(2,1)}) %reduce-scatter.2.cloned.1.call-update) | async-done | bytes 524304 | tf_op jit(solution)/shard_map/reduce_scatter | solution.py:106
  308.2 0.0 copy-done.1
  (16 shorter events, 0.1 us)
Async XLA Ops:
  6.5 1.6 copy-start
  6.5 6.3 %copy-start.3 = (s32[32,32]{1,0:T(8,128)S(1)}, s32[32,32]{1,0:T(8,128)}, u32[]{:S(2)}) copy-start(s32[32,32]{1,0:T(8,128)} %param.13) | copy-start | bytes 12292
  6.5 43.6 %all-gather.2.cloned.1.call-start = ((), (), s32[]{:S(2)}) async-start(), calls=%async_computation.1 | async-start | bytes 5242880 | tf_op jit(solution)/shard_map/all_gather | solution.py:97
  12.8 295.4 %reduce-scatter.2.cloned.1.call-start = ((), (), s32[]{:S(2)}) async-start(), calls=%async_computation.2 | async-start | bytes 2621440 | tf_op jit(solution)/shard_map/reduce_scatter | solution.py:106
  20.7 36.0 %copy-start.2 = (bf16[1024,256]{1,0:T(8,128)(2,1)S(1)}, bf16[1024,256]{1,0:T(8,128)(2,1)}, u32[]{:S(2)}) copy-start(bf16[1024,256]{1,0:T(8,128)(2,1)} %convolution_convert_fusion.1) | copy-start | bytes 1572868
  158.8 149.5 %copy-start.1 = (bf16[1024,1024]{1,0:T(8,128)(2,1)S(1)}, bf16[1024,1024]{1,0:T(8,128)(2,1)}, u32[]{:S(2)}) copy-start(bf16[1024,1024]{1,0:T(8,128)(2,1)} %param.8) | copy-start | bytes 6291460
Sparse Core Ops, SparseCore 0:
  12.9 37.1 all-gather.1
  162.7 145.4 reduce-scatter.1
where the time goes:
time: 317 us; the launch traced here: 315 us
  waiting for transfers between devices  175 us (55%)
  local copies, waits for them, and re-layouts  46.2 us (15%)
  other arithmetic  42.8 us (14%)
  matrix products  36.2 us (11%)
  between operations  14.2 us (4%)
    reduce_scatter x1, waiting for transfers between devices, on_device(): lax.psum_scatter(jnp.dot(attended, w_out, preferred_element_type=jnp.floa...  146 us
    all_gather x1, waiting for transfers between devices, on_device(): lax.all_gather(key_value, 'band', axis=0, tiled=True)  29.4 us
    dot_general x1, matrix products, one_turn(): jnp.einsum('prhk,pkhd->prhd', weights, value_rows, preferred_element_type...  14.6 us
    slice x2, local copies, waits for them, and re-layouts, one_turn(): pair_rows[:, :, local_cols:].reshape(per_turn, -1, head_count, head_dim)  12.4 us
    scatter-add x1, other arithmetic, one_turn(): jax.ops.segment_sum(sum_terms, owners, num_segments=item_count)  12.3 us
    dot_general x1, matrix products, one_turn(): jnp.einsum('prhd,pkhd->prhk', query_rows, key_rows, preferred_element_typ...  12.2 us
    reduce_sum x1, other arithmetic, one_turn(): row_mass = jnp.sum(exponent, axis=3)  10.7 us
    gather x2, local copies, waits for them, and re-layouts, one_turn(): jnp.take(item_rows, owners, axis=0)  9.12 us
  transfers between devices with their start and end apart: 2, of which 2 were waited for; matrix products, arithmetic and copies ran while one was open for 2% of the time, Pallas kernels for 0%

commit v1 on v0

v1 whole, which is shorter than its diff:
```python
import functools
import jax
import jax.numpy as jnp
from jax import lax
from jax.experimental import pallas as pl
from jax.experimental.pallas import tpu as pltpu
from jax.sharding import PartitionSpec as P

HD = 64
BLK = 128
KEEP = 6
UNROLL = 4
LOW = -1e30
SCALE = HD**-0.5 * 1.4426950408889634
MIB = 1 << 20
BF16 = jnp.bfloat16
F32 = jnp.float32
NT = (((1,), (1,)), ((), ()))
TN = (((0,), (0,)), ((), ()))


def greet(peers):
    barrier = pltpu.get_barrier_semaphore()
    for peer in peers:
        pl.semaphore_signal(barrier, inc=1, device_id=peer, device_id_type=pl.DeviceIdType.MESH)
    pl.semaphore_wait(barrier, len(peers))


def project_exchange(nb, nh, sel, tok, wq, wk, wv, q_all, kv_all, qs, kvs, send_kv, recv_kv, send_q, recv_q, own):
    me = lax.axis_index("band")
    group, place = me // nh, lax.rem(me, nh)
    nq = tok.shape[0]
    others = [lax.rem(me + d, nb) for d in range(1, nb)]
    greet([{"band": p} for p in others])

    for k in range(KEEP):
        rows = tok[sel[k]]
        keys = jnp.dot(rows, wk[...], preferred_element_type=F32)
        vals = jnp.dot(rows, wv[...], preferred_element_type=F32)
        for h in range(nh):
            cut = slice(h * HD, (h + 1) * HD)
            kvs[h, k] = jnp.concatenate([keys[:, cut], vals[:, cut]], axis=1).astype(BF16)

    def kv_copy(peer, origin):
        return pltpu.make_async_remote_copy(
            src_ref=kvs.at[lax.rem(peer, nh)],
            dst_ref=kv_all.at[pl.ds(origin * KEEP, KEEP)],
            send_sem=send_kv.at[peer],
            recv_sem=recv_kv.at[origin],
            device_id={"band": peer},
            device_id_type=pl.DeviceIdType.MESH,
        )

    order = [p for _, p in sorted(zip([abs(d - nb // 2) for d in range(1, nb)], range(nb - 1)))]
    for i in order:
        kv_copy(others[i], me).start()
    own_kv = pltpu.make_async_copy(kvs.at[place], kv_all.at[pl.ds(me * KEEP, KEEP)], own.at[0])
    own_kv.start()

    for m in range(nq // 2):
        two = jnp.dot(
            jnp.concatenate([tok[2 * m], tok[2 * m + 1]], axis=0), wq[...], preferred_element_type=F32
        )
        for h in range(nh):
            cut = slice(h * HD, (h + 1) * HD)
            qs[h, m] = jnp.concatenate([two[:BLK, cut], two[BLK:, cut]], axis=1).astype(BF16)

    def q_copy(to, origin):
        return pltpu.make_async_remote_copy(
            src_ref=qs.at[to],
            dst_ref=q_all.at[origin],
            send_sem=send_q.at[to],
            recv_sem=recv_q.at[origin],
            device_id={"band": group * nh + to},
            device_id_type=pl.DeviceIdType.MESH,
        )

    mates = [lax.rem(place + d, nh) for d in range(1, nh)]
    order_q = [i for _, i in sorted(zip([abs(d - nh // 2) for d in range(1, nh)], range(nh - 1)))]
    for i in order_q:
        q_copy(mates[i], place).start()
    own_q = pltpu.make_async_copy(qs.at[place], q_all.at[place], own.at[1])
    own_q.start()
    own_kv.wait()
    own_q.wait()
    for p in others:
        kv_copy(p, me).wait_send()
        kv_copy(p, p).wait_recv()
    for p in mates:
        q_copy(p, place).wait_send()
        q_copy(p, p).wait_recv()


def attend(work, turns, q_in, kv, out, q_pad, v_t):
    n_kv, n_pair = kv.shape[0], q_in.shape[0]
    lane = lax.broadcasted_iota(jnp.int32, (BLK, BLK), 1)

    def prepare_kv(c, _):
        v_t[c] = kv[c].T[HD:]
        return 0

    lax.fori_loop(0, n_kv, prepare_kv, 0, unroll=4)

    def prepare_q(m, _):
        two = q_in[m].astype(F32)
        q_pad[2 * m] = jnp.where(lane < HD, two, 0.0).astype(BF16)
        q_pad[2 * m + 1] = jnp.where(lane < HD, pltpu.roll(two, HD, 1), 0.0).astype(BF16)
        return 0

    lax.fori_loop(0, n_pair, prepare_q, 0, unroll=2)
    q_pad[2 * n_pair] = jnp.zeros((BLK, BLK), BF16)

    def turn(i, state):
        peak, mass, total = state
        parts = []
        for u in range(UNROLL):
            t = i * UNROLL + u
            q, a, b = work[0, t], work[1, t], work[2, t]
            scores = lax.dot_general(
                jnp.concatenate([kv[a], kv[b]], axis=0), q_pad[q], NT, preferred_element_type=F32
            ) * SCALE
            bias = jnp.where(work[3, t] > 0, 0.0, LOW)
            scores = jnp.concatenate([scores[:BLK], scores[BLK:] + bias], axis=0)
            top = jnp.max(scores, axis=0, keepdims=True)
            weight = jnp.exp2(scores - top)
            part = jnp.sum(weight, axis=0, keepdims=True)
            values = jnp.concatenate([v_t[a], v_t[b]], axis=1)
            got = jnp.dot(values, weight.astype(BF16), preferred_element_type=F32)
            parts.append((q, work[4, t], top, part, got))
        for q, first, top, part, got in parts:
            before = jnp.where(first > 0, LOW, peak)
            peak = jnp.maximum(before, top)
            f, g = jnp.exp2(before - peak), jnp.exp2(top - peak)
            mass = mass * f + part * g
            total = total * f + got * g
            out[q] = (total / mass).astype(BF16)
        return peak, mass, total

    start = (jnp.full((1, BLK), LOW, F32), jnp.zeros((1, BLK), F32), jnp.zeros((HD, BLK), F32))
    lax.fori_loop(0, turns[0], turn, start)


def exchange_project(nh, nz, att, w_full, out, got, send, recv, own):
    band, z = lax.axis_index("band"), lax.axis_index("head")
    group, place = band // nh, lax.rem(band, nh)
    n = nh * nz
    me = z * nh + place
    per = got.shape[1]
    per_band = per * nz
    others = [lax.rem(me + d, n) for d in range(1, n)]
    where = lambda p: {"band": group * nh + lax.rem(p, nh), "head": p // nh}
    greet([where(p) for p in others])

    def piece(p):
        return att.at[pl.ds(lax.rem(p, nh) * per_band + (p // nh) * per, per)]

    def copy(peer, origin):
        return pltpu.make_async_remote_copy(
            src_ref=piece(peer),
            dst_ref=got.at[origin],
            send_sem=send.at[peer],
            recv_sem=recv.at[origin],
            device_id=where(peer),
            device_id_type=pl.DeviceIdType.MESH,
        )

    for _, i in sorted(zip([abs(d - n // 2) for d in range(1, n)], range(n - 1))):
        copy(others[i], me).start()
    mine = pltpu.make_async_copy(piece(me), got.at[me], own.at[0])
    mine.start()
    mine.wait()
    for p in others:
        copy(p, me).wait_send()
        copy(p, p).wait_recv()
    for r in range(per):
        heads = jnp.concatenate([got[i, r] for i in range(n)], axis=0)
        out[pl.ds(r * BLK, BLK), :] = lax.dot_general(
            heads, w_full[...], TN, preferred_element_type=F32
        ).astype(BF16)


def plan(block_mask, nb, nh, me):
    n_kb = block_mask.shape[1]
    per_band = n_kb // nb
    nq = per_band * nh
    i32 = jnp.int32
    named = jnp.max(block_mask, axis=0).reshape(nb, per_band)
    low = jnp.arange(per_band)[:, None] < jnp.arange(per_band)[None, :]
    rank = jnp.sum(named[:, :, None] * low[None].astype(i32), axis=1)
    place = (jnp.arange(nb, dtype=i32)[:, None] * KEEP + jnp.minimum(rank, KEEP - 1)).reshape(-1)
    hit = (named[:, None, :] > 0) & (rank[:, None, :] == jnp.arange(KEEP)[None, :, None])
    sel_all = jnp.sum(jnp.where(hit, jnp.arange(per_band, dtype=i32)[None, None, :], 0), axis=2)
    sel = lax.dynamic_index_in_dim(sel_all, me, 0, keepdims=False)
    rows = lax.dynamic_slice_in_dim(block_mask, (me // nh) * nq, nq, 0)
    below = (jnp.arange(n_kb)[:, None] < jnp.arange(n_kb)[None, :]).astype(i32)
    pos = jnp.sum(rows[:, :, None] * below[None], axis=1)
    chunks = (jnp.sum(rows, axis=1) + 1) // 2
    upto = (jnp.arange(nq)[:, None] <= jnp.arange(nq)[None, :]).astype(i32)
    end = jnp.sum(chunks[:, None] * upto, axis=0)
    begin = end - chunks
    t_max = nq * ((nb * KEEP + 1) // 2)
    t_max = -(-t_max // UNROLL) * UNROLL
    t = jnp.arange(t_max, dtype=i32)
    slot = (begin[:, None] * 2 + pos).reshape(-1)[:, None]
    kept = (rows.reshape(-1) > 0)[:, None]
    key = jnp.tile(place, nq)[:, None]
    even = kept & (slot == 2 * t[None])
    odd = kept & (slot == 2 * t[None] + 1)
    work = jnp.stack(
        [
            jnp.sum((end[:, None] <= t[None]).astype(i32), axis=0),
            jnp.sum(jnp.where(even, key, 0), axis=0),
            jnp.sum(jnp.where(odd, key, 0), axis=0),
            jnp.sum(odd.astype(i32), axis=0),
            jnp.sum((begin[:, None] == t[None]).astype(i32), axis=0),
        ]
    )
    turns = (end[-1:] + UNROLL - 1) // UNROLL
    return sel, work, turns


def on_device(nb, nz, tokens, w_query, w_key, w_value, w_out, block_mask):
    me = lax.axis_index("band")
    nh = w_query.shape[1] // HD
    tok_rows = tokens.shape[0]
    nq = tok_rows // BLK
    per = nq // nz
    vmem = pl.BlockSpec(memory_space=pltpu.VMEM)
    smem = pl.BlockSpec(memory_space=pltpu.SMEM)
    hbm = pl.BlockSpec(memory_space=pl.ANY)
    dma = pltpu.SemaphoreType.DMA
    w_full = lax.all_gather(w_out, "head", axis=0, tiled=True)
    sel, work, turns = plan(block_mask, nb, nh, me)
    q_all, kv_all = pl.pallas_call(
        functools.partial(project_exchange, nb, nh),
        out_shape=(
            jax.ShapeDtypeStruct((nh, nq // 2, BLK, BLK), BF16),
            jax.ShapeDtypeStruct((nb * KEEP, BLK, BLK), BF16),
        ),
        in_specs=[smem, vmem, vmem, vmem, vmem],
        out_specs=(hbm, hbm),
        scratch_shapes=[
            pltpu.VMEM((nh, nq // 2, BLK, BLK), BF16),
            pltpu.VMEM((nh, KEEP, BLK, BLK), BF16),
            dma((nb,)),
            dma((nb,)),
            dma((nh,)),
            dma((nh,)),
            dma((2,)),
        ],
        compiler_params=pltpu.CompilerParams(
            collective_id=0, has_side_effects=True, vmem_limit_bytes=32 * MIB
        ),
        name="project_exchange",
    )(sel, tokens.reshape(nq, BLK, -1), w_query, w_key, w_value)
    att = pl.pallas_call(
        attend,
        out_shape=jax.ShapeDtypeStruct((nh * nq + 1, HD, BLK), BF16),
        in_specs=[smem, smem, vmem, vmem],
        out_specs=vmem,
        scratch_shapes=[
            pltpu.VMEM((nh * nq + 1, BLK, BLK), BF16),
            pltpu.VMEM((nb * KEEP, HD, BLK), BF16),
        ],
        compiler_params=pltpu.CompilerParams(vmem_limit_bytes=32 * MIB),
        name="attend",
    )(work, turns, q_all.reshape(nh * nq // 2, BLK, BLK), kv_all)
    n = nh * nz
    return pl.pallas_call(
        functools.partial(exchange_project, nh, nz),
        out_shape=jax.ShapeDtypeStruct((per * BLK, w_out.shape[1]), BF16),
        in_specs=[hbm, vmem],
        out_specs=vmem,
        scratch_shapes=[
            pltpu.VMEM((n, per, HD, BLK), BF16),
            dma((n,)),
            dma((n,)),
            dma((1,)),
        ],
        compiler_params=pltpu.CompilerParams(
            collective_id=1, has_side_effects=True, vmem_limit_bytes=32 * MIB
        ),
        name="exchange_project",
    )(att, w_full)


def solution(mesh):
    return jax.shard_map(
        functools.partial(on_device, mesh.shape["band"], mesh.shape["head"]),
        mesh=mesh,
        in_specs=(
            P(("tiles", "band"), None),
            P(None, "head"),
            P(None, "head"),
            P(None, "head"),
            P("head", None),
            P("tiles", None),
        ),
        out_specs=P(("tiles", "band", "head"), None),
        check_vma=False,
    )
```

time: 317 us -> 97.3 us (0.31); the launches traced: 315 us -> 98.6 us
  waiting for transfers between devices: 175 us -> 0.73 us
  Pallas kernels: 0 us -> 71.2 us
  other arithmetic: 42.8 us -> 4.15 us
  local copies, waits for them, and re-layouts: 46.2 us -> 8.35 us
  matrix products: 36.2 us -> 0 us
    reduce_scatter x1 -> x0, waiting for transfers between devices: 146 us -> none  [on_device(): lax.psum_scatter(jnp.dot(attended, w_out, preferred_element_type=jnp.floa...]
    pallas_call x0 -> x3, Pallas kernels: none -> 71.2 us  [the longest x1 34.1 us: on_device(): pl.pallas_call(attend, out_shape=jax.ShapeDtypeStruct((nh * nq + 1, HD, B...]
    dot_general x6 -> x0, matrix products: 36.2 us -> none  [the longest x1 14.6 us: one_turn(): jnp.einsum('prhk,pkhd->prhd', weights, value_rows, preferred_element_type...]
    all_gather x1, waiting for transfers between devices: 29.4 us -> 0.02 us  [on_device(): w_full = lax.all_gather(w_out, 'head', axis=0, tiled=True)]
    gather x6 -> x0, local copies, waits for them, and re-layouts: 18.8 us -> none  [the longest x2 9.12 us: one_turn(): jnp.take(item_rows, owners, axis=0)]
    slice x3 -> x1, local copies, waits for them, and re-layouts: 18.8 us -> 0.59 us  [plan(): turns = (end[-1:] + UNROLL - 1) // UNROLL]
    scatter-add x2 -> x0, other arithmetic: 15.2 us -> none  [the longest x1 12.3 us: one_turn(): jax.ops.segment_sum(sum_terms, owners, num_segments=item_count)]
    reduce_sum x1 -> x7, other arithmetic: 10.7 us -> 2.38 us  [the longest x1 0.94 us: plan(): pos = jnp.sum(rows[:, :, None] * below[None], axis=1)]
  transfers between devices with their start and end apart: 2 -> 1, of which waited for: 2 -> 0; matrix products, arithmetic and copies ran while one was open for 2% -> 5% of each run, Pallas kernels for 0% -> 55%
where the time goes in v1:
time: 97.3 us; the launch traced here: 98.6 us
  Pallas kernels  71.2 us (73%)
  between operations  14.2 us (15%)
  local copies, waits for them, and re-layouts  8.35 us (9%)
  other arithmetic  4.15 us (4%)
    pallas_call x1, Pallas kernels, on_device(): pl.pallas_call(attend, out_shape=jax.ShapeDtypeStruct((nh * nq + 1, HD, B...  34.1 us
    pallas_call x1, Pallas kernels, on_device(): pl.pallas_call(functools.partial(project_exchange, nb, nh), out_shape=(ja...  20 us
    pallas_call x1, Pallas kernels, on_device(): pl.pallas_call(functools.partial(exchange_project, nh, nz), out_shape=jax...  17.1 us
    unnamed x11, local copies, waits for them, and re-layouts  7.12 us
  transfers between devices with their start and end apart: 1, of which 0 were waited for; matrix products, arithmetic and copies ran while one was open for 5% of the time, Pallas kernels for 55%

profile of v1, /device:TPU:0, one launch (start us, length us, event | category | flops | bytes accessed | tf_op | source)
XLA Modules:
  0.0 98.6 jit_solution(8672717177688836891)
XLA Ops:
  6.5 0.0 all-gather.2.cloned.1.call-start
  6.5 0.7 all-gather.2.cloned.1.call-update
  7.3 0.8 fusion.3
  8.1 0.1 select_reduce_fusion.2
  8.2 0.6 slice.3
  9.5 0.9 multiply_reduce_fusion
  10.4 0.1 broadcast_add_fusion
  10.5 0.1 add.83
  10.6 0.1 mul.79
  10.7 0.1 multiply_reduce_fusion.1
  10.8 0.1 minimum_add_fusion
  10.8 0.1 add.86
  10.9 0.1 broadcast_in_dim.26
  11.0 0.7 broadcast_compare_fusion
  11.7 0.1 gt.23
  11.8 0.9 select_reduce_fusion
  12.8 0.1 convert_reduce_fusion.1
  12.9 0.1 convert_reduce_fusion.2
  13.0 0.2 select_reduce_fusion.3
  13.2 0.2 dynamic-slice_reduce_fusion.sel
  13.4 0.0 copy-start.1
  13.4 1.6 %copy-done.1 = bf16[1024,1024]{1,0:T(8,128)(2,1)S(1)} copy-done((bf16[1024,1024]{1,0:T(8,128)(2,1)S(1)}, bf16[1024,1024]{1,0:T(8,128)(2,1)}, u32[]{:S(2)}) %copy-start.1) | copy-done | bytes 2097176
  15.0 0.0 copy-start.2
  15.0 1.0 %copy-done.2 = bf16[1024,256]{1,0:T(8,128)(2,1)S(1)} copy-done((bf16[1024,256]{1,0:T(8,128)(2,1)S(1)}, bf16[1024,256]{1,0:T(8,128)(2,1)}, u32[]{:S(2)}) %copy-start.2) | copy-done | bytes 524312
  16.0 0.0 copy-start.3
  16.0 1.0 %copy-done.3 = bf16[1024,256]{1,0:T(8,128)(2,1)S(1)} copy-done((bf16[1024,256]{1,0:T(8,128)(2,1)S(1)}, bf16[1024,256]{1,0:T(8,128)(2,1)}, u32[]{:S(2)}) %copy-start.3) | copy-done | bytes 524312
  17.1 0.0 copy-start.4
  17.1 1.1 %copy-done.4 = bf16[1024,256]{1,0:T(8,128)(2,1)S(1)} copy-done((bf16[1024,256]{1,0:T(8,128)(2,1)S(1)}, bf16[1024,256]{1,0:T(8,128)(2,1)}, u32[]{:S(2)}) %copy-start.4) | copy-done | bytes 524312
  18.1 20.0 %project_exchange.1 = (bf16[4,4,128,128]{3,2,1,0:T(8,128)(2,1)S(1)}, bf16[24,128,128]{2,1,0:T(8,128)(2,1)S(1)}) custom-call(s32[6]{0:T(128)S(1)} %dynamic-slice_reduce_fusion.sel, bf16[8,128,1024]{2,1,0:T(8,128)(2,1)S(1)} %bitcast.2, bf16[1024,256]{1,0:T(8,128)(2,1)S(1)} %copy-done.2, bf16[1024,256]{1,0:T(8,128)(2,1)S(1)} %copy-done.3, ...), custom_call_target="tpu_custom_call" | custom-call | tf_op jit(solution)/shard_map/project_exchange/pallas_call | solution.py:234
  38.1 34.1 %attend.1.att = bf16[33,64,128]{2,1,0:T(8,128)(2,1)S(1)} custom-call(s32[5,384]{1,0:T(8,128)S(1)} %stack.23.work, s32[1]{0:T(128)S(6)} %select_n.42.turns, bf16[16,128,128]{2,1,0:T(8,128)(2,1)S(1)} %bitcast.3, bf16[24,128,128]{2,1,0:T(8,128)(2,1)S(1)} %get-tuple-element.8.kv), custom_call_target="tpu_custom_call" | custom-call | tf_op jit(solution)/shard_map/attend/pallas_call | solution.py:256
  72.2 0.0 all-gather.2.cloned.1.call-done.w_full
  72.2 0.0 copy-start
  72.2 1.6 %copy-done = bf16[1024,1024]{1,0:T(8,128)(2,1)S(1)} copy-done((bf16[1024,1024]{1,0:T(8,128)(2,1)S(1)}, bf16[1024,1024]{1,0:T(8,128)(2,1)}, u32[]{:S(2)}) %copy-start) | copy-done | bytes 2097176
  73.8 17.1 %exchange_project.1 = bf16[256,1024]{1,0:T(8,128)(2,1)S(1)} custom-call(bf16[33,64,128]{2,1,0:T(8,128)(2,1)S(1)} %attend.1.att, bf16[1024,1024]{1,0:T(8,128)(2,1)S(1)} %copy-done), custom_call_target="tpu_custom_call" | custom-call | tf_op jit(solution)/shard_map/exchange_project/pallas_call | solution.py:269
  90.9 0.8 copy.8
  (14 shorter events, 0.1 us)
Async XLA Ops:
  6.5 65.7 %all-gather.2.cloned.1.call-start = ((), (), s32[]{:S(2)}) async-start(), calls=%async_computation | async-start | bytes 2621440 | tf_op jit(solution)/shard_map/all_gather | solution.py:232
  13.4 1.6 %copy-start.1 = (bf16[1024,1024]{1,0:T(8,128)(2,1)S(1)}, bf16[1024,1024]{1,0:T(8,128)(2,1)}, u32[]{:S(2)}) copy-start(bf16[1024,1024]{1,0:T(8,128)(2,1)} %param.6) | copy-start | bytes 6291460
  15.0 1.0 %copy-start.2 = (bf16[1024,256]{1,0:T(8,128)(2,1)S(1)}, bf16[1024,256]{1,0:T(8,128)(2,1)}, u32[]{:S(2)}) copy-start(bf16[1024,256]{1,0:T(8,128)(2,1)} %wq.1) | copy-start | bytes 1572868
  16.0 1.0 %copy-start.3 = (bf16[1024,256]{1,0:T(8,128)(2,1)S(1)}, bf16[1024,256]{1,0:T(8,128)(2,1)}, u32[]{:S(2)}) copy-start(bf16[1024,256]{1,0:T(8,128)(2,1)} %wk.1) | copy-start | bytes 1572868
  17.1 1.1 %copy-start.4 = (bf16[1024,256]{1,0:T(8,128)(2,1)S(1)}, bf16[1024,256]{1,0:T(8,128)(2,1)}, u32[]{:S(2)}) copy-start(bf16[1024,256]{1,0:T(8,128)(2,1)} %wv.1) | copy-start | bytes 1572868
  72.2 1.6 %copy-start = (bf16[1024,1024]{1,0:T(8,128)(2,1)S(1)}, bf16[1024,1024]{1,0:T(8,128)(2,1)}, u32[]{:S(2)}) copy-start(bf16[1024,1024]{1,0:T(8,128)(2,1)} %all-gather.2.cloned.1.call-done.w_full) | copy-start | bytes 6291460
Sparse Core Ops, SparseCore 0:
  8.9 48.7 all-gather.1

commit v2 on v1

v2 whole, which is shorter than its diff:
```python
import functools
import jax
import jax.numpy as jnp
from jax import lax
from jax.experimental import pallas as pl
from jax.experimental.pallas import tpu as pltpu
from jax.sharding import PartitionSpec as P

HD = 64
BLK = 128
KEEP = 6
UNROLL = 4
LOW = -1e30
SCALE = HD**-0.5 * 1.4426950408889634
MIB = 1 << 20
BF16 = jnp.bfloat16
F32 = jnp.float32
NT = (((1,), (1,)), ((), ()))
TN = (((0,), (0,)), ((), ()))


def greet(peers):
    barrier = pltpu.get_barrier_semaphore()
    for peer in peers:
        pl.semaphore_signal(barrier, inc=1, device_id=peer, device_id_type=pl.DeviceIdType.MESH)


def all_greeted(peers):
    pl.semaphore_wait(pltpu.get_barrier_semaphore(), len(peers))


def make_plan(mask, group, nb, nh, work, turns):
    n_rows, n_kb = mask.shape
    per_band = n_kb // nb
    nq = per_band * nh
    t_max = work.shape[1]
    i32 = jnp.int32
    everything = mask[...].astype(F32)
    rows = mask[pl.ds(group * nq, nq), :].astype(F32)
    named = jnp.max(everything, axis=0, keepdims=True)
    left = lax.broadcasted_iota(i32, (n_kb, n_kb), 0)
    right = lax.broadcasted_iota(i32, (n_kb, n_kb), 1)
    below = (left < right).astype(F32)
    same = (left // per_band == right // per_band).astype(F32)
    rank = jnp.dot(named, below * same, preferred_element_type=F32)
    band = (lax.broadcasted_iota(i32, (1, n_kb), 1) // per_band).astype(F32)
    key = band * KEEP + jnp.minimum(rank, KEEP - 1.0)
    pos = jnp.dot(rows, below, preferred_element_type=F32)
    count = jnp.sum(rows, axis=1, keepdims=True)
    chunks = jnp.floor((count + 1.0) * 0.5)
    qi = lax.broadcasted_iota(i32, (nq, nq), 0)
    qj = lax.broadcasted_iota(i32, (nq, nq), 1)
    begin = jnp.dot(
        (qj < qi).astype(F32), jnp.broadcast_to(chunks, (nq, 128)),
        preferred_element_type=F32, precision=lax.Precision.HIGHEST,
    )[:, :1]
    end = begin + chunks
    slot = jnp.where(rows > 0, begin * 2.0 + pos, -1.0).T
    keys = jnp.broadcast_to(key, (nq, n_kb)).T
    t = lax.broadcasted_iota(i32, (1, t_max), 1).astype(F32)
    first_key = jnp.zeros((n_kb, t_max), F32)
    second_key = jnp.zeros((n_kb, t_max), F32)
    has_second = jnp.zeros((n_kb, t_max), F32)
    for q in range(nq):
        at, value = slot[:, q : q + 1], keys[:, q : q + 1]
        even, odd = at == 2.0 * t, at == 2.0 * t + 1.0
        first_key = first_key + jnp.where(even, value, 0.0)
        second_key = second_key + jnp.where(odd, value, 0.0)
        has_second = has_second + jnp.where(odd, 1.0, 0.0)
    total = lambda x: jnp.sum(x, axis=0, keepdims=True)
    a, b, two = total(first_key), total(second_key), total(has_second)
    work[0:1, :] = total((end <= t).astype(F32)).astype(i32)
    work[1:2, :] = a.astype(i32)
    work[2:3, :] = jnp.where(two > 0, b, a).astype(i32)
    work[3:4, :] = total((begin == t).astype(F32)).astype(i32)
    work[4:5, :] = (1.0 - two).astype(i32)
    work[5:8, :] = jnp.zeros((3, t_max), i32)
    turns[...] = jnp.broadcast_to(
        jnp.floor((jnp.sum(chunks, axis=0, keepdims=True) + (UNROLL - 1.0)) * (1.0 / UNROLL)), (8, 128)
    ).astype(i32)


def select_blocks(mask, me, per_band):
    named = []
    for i in range(per_band):
        named.append(
            functools.reduce(jnp.maximum, [mask[r, me * per_band + i] for r in range(mask.shape[0])])
        )
    picks, rank = [0] * KEEP, 0
    for i in range(per_band):
        for k in range(min(i + 1, KEEP)):
            picks[k] = picks[k] + i * named[i] * (rank == k)
        rank = rank + named[i]
    return picks


def project_exchange(
    nb, nh, mask_s, mask_v, tok_hbm, wq_hbm, wk_hbm, wv_hbm,
    q_all, kv_all, work, turns,
    tok, wq, wk, wv, qs, kvs, send_kv, recv_kv, send_q, recv_q, own, load,
):
    loads = [
        pltpu.make_async_copy(a, b, load.at[i])
        for i, (a, b) in enumerate(((wk_hbm, wk), (wv_hbm, wv), (tok_hbm, tok), (wq_hbm, wq)))
    ]
    for c in loads:
        c.start()
    me = lax.axis_index("band")
    group, place = me // nh, lax.rem(me, nh)
    nq = tok.shape[0]
    others = [lax.rem(me + d, nb) for d in range(1, nb)]
    greet([{"band": p} for p in others])
    sel = select_blocks(mask_s, me, nq)
    for c in loads[:3]:
        c.wait()

    for k in range(KEEP):
        rows = tok[sel[k]]
        keys = jnp.dot(rows, wk[...], preferred_element_type=F32)
        vals = jnp.dot(rows, wv[...], preferred_element_type=F32)
        for h in range(nh):
            cut = slice(h * HD, (h + 1) * HD)
            kvs[h, k] = jnp.concatenate([keys[:, cut], vals[:, cut]], axis=1).astype(BF16)
    all_greeted(others)

    def kv_copy(peer, origin):
        return pltpu.make_async_remote_copy(
            src_ref=kvs.at[lax.rem(peer, nh)],
            dst_ref=kv_all.at[pl.ds(origin * KEEP, KEEP)],
            send_sem=send_kv.at[peer],
            recv_sem=recv_kv.at[origin],
            device_id={"band": peer},
            device_id_type=pl.DeviceIdType.MESH,
        )

    order = [p for _, p in sorted(zip([abs(d - nb // 2) for d in range(1, nb)], range(nb - 1)))]
    for i in order:
        kv_copy(others[i], me).start()
    own_kv = pltpu.make_async_copy(kvs.at[place], kv_all.at[pl.ds(me * KEEP, KEEP)], own.at[0])
    own_kv.start()

    loads[3].wait()
    for m in range(nq // 2):
        two = jnp.dot(
            jnp.concatenate([tok[2 * m], tok[2 * m + 1]], axis=0), wq[...], preferred_element_type=F32
        )
        for h in range(nh):
            cut = slice(h * HD, (h + 1) * HD)
            qs[h, m] = jnp.concatenate([two[:BLK, cut], two[BLK:, cut]], axis=1).astype(BF16)

    def q_copy(to, origin):
        return pltpu.make_async_remote_copy(
            src_ref=qs.at[to],
            dst_ref=q_all.at[origin],
            send_sem=send_q.at[to],
            recv_sem=recv_q.at[origin],
            device_id={"band": group * nh + to},
            device_id_type=pl.DeviceIdType.MESH,
        )

    mates = [lax.rem(place + d, nh) for d in range(1, nh)]
    order_q = [i for _, i in sorted(zip([abs(d - nh // 2) for d in range(1, nh)], range(nh - 1)))]
    for i in order_q:
        q_copy(mates[i], place).start()
    own_q = pltpu.make_async_copy(qs.at[place], q_all.at[place], own.at[1])
    own_q.start()
    make_plan(mask_v, group, nb, nh, work, turns)
    own_kv.wait()
    own_q.wait()
    for p in others:
        kv_copy(p, me).wait_send()
        kv_copy(p, p).wait_recv()
    for p in mates:
        q_copy(p, place).wait_send()
        q_copy(p, p).wait_recv()


def attend(work, turns, q_in, kv, out, q_pad, v_t):
    n_kv, n_pair = kv.shape[0], q_in.shape[0]

    def prepare_kv(c, _):
        v_t[c] = kv[c].T[HD:]
        return 0

    lax.fori_loop(0, n_kv, prepare_kv, 0, unroll=4)
    zeros = jnp.zeros((HD, BLK), BF16)

    def prepare_q(m, _):
        two = q_in[m].T
        q_pad[2 * m] = jnp.concatenate([two[:HD], zeros], axis=0)
        q_pad[2 * m + 1] = jnp.concatenate([two[HD:], zeros], axis=0)
        return 0

    lax.fori_loop(0, n_pair, prepare_q, 0, unroll=2)
    q_pad[2 * n_pair] = jnp.zeros((BLK, BLK), BF16)

    def turn(i, state):
        peak, mass, total = state
        parts = []
        for u in range(UNROLL):
            t = i * UNROLL + u
            q, pair = work[0, t], (work[1, t], work[2, t])
            scores = [jnp.dot(kv[c], q_pad[q], preferred_element_type=F32) * SCALE for c in pair]
            top = functools.reduce(jnp.maximum, [jnp.max(x, axis=0, keepdims=True) for x in scores])
            weights = [jnp.exp2(x - top) for x in scores]
            part = functools.reduce(jnp.add, [jnp.sum(x, axis=0, keepdims=True) for x in weights])
            got = functools.reduce(
                jnp.add,
                [jnp.dot(v_t[c], x.astype(BF16), preferred_element_type=F32) for c, x in zip(pair, weights)],
            )
            parts.append((q, work[3, t], work[4, t], top, part, got))
        for q, first, repeat, top, part, got in parts:
            before = jnp.where(first > 0, LOW, peak)
            peak = jnp.maximum(before, top)
            f = jnp.exp2(before - peak)
            g = jnp.exp2(top - peak) * jnp.where(repeat > 0, 0.5, 1.0)
            mass = mass * f + part * g
            total = total * f + got * g
            out[q] = (total * (1.0 / mass)).astype(BF16)
        return peak, mass, total

    start = (jnp.full((1, BLK), LOW, F32), jnp.zeros((1, BLK), F32), jnp.zeros((HD, BLK), F32))
    lax.fori_loop(0, turns[0, 0], turn, start)


def exchange_project(nh, nz, att, w_hbm, out, got, w_full, send, recv, own):
    band, z = lax.axis_index("band"), lax.axis_index("head")
    group, place = band // nh, lax.rem(band, nh)
    n = nh * nz
    me = z * nh + place
    per = got.shape[1]
    per_band = per * nz
    others = [lax.rem(me + d, n) for d in range(1, n)]
    where = lambda p: {"band": group * nh + lax.rem(p, nh), "head": p // nh}
    w_load = pltpu.make_async_copy(w_hbm, w_full, own.at[1])
    w_load.start()
    greet([where(p) for p in others])
    all_greeted(others)

    def piece(p):
        return att.at[pl.ds(lax.rem(p, nh) * per_band + (p // nh) * per, per)]

    def copy(peer, origin):
        return pltpu.make_async_remote_copy(
            src_ref=piece(peer),
            dst_ref=got.at[origin],
            send_sem=send.at[peer],
            recv_sem=recv.at[origin],
            device_id=where(peer),
            device_id_type=pl.DeviceIdType.MESH,
        )

    for _, i in sorted(zip([abs(d - n // 2) for d in range(1, n)], range(n - 1))):
        copy(others[i], me).start()
    mine = pltpu.make_async_copy(piece(me), got.at[me], own.at[0])
    mine.start()
    mine.wait()
    w_load.wait()
    for p in others:
        copy(p, me).wait_send()
        copy(p, p).wait_recv()
    for r in range(per):
        heads = jnp.concatenate([got[i, r] for i in range(n)], axis=0)
        out[pl.ds(r * BLK, BLK), :] = lax.dot_general(
            heads, w_full[...], TN, preferred_element_type=F32
        ).astype(BF16)


def on_device(nb, nz, tokens, w_query, w_key, w_value, w_out, block_mask):
    nh = w_query.shape[1] // HD
    tok_rows = tokens.shape[0]
    nq = tok_rows // BLK
    per = nq // nz
    vmem = pl.BlockSpec(memory_space=pltpu.VMEM)
    smem = pl.BlockSpec(memory_space=pltpu.SMEM)
    hbm = pl.BlockSpec(memory_space=pl.ANY)
    dma = pltpu.SemaphoreType.DMA
    w_full = lax.all_gather(w_out, "head", axis=0, tiled=True)
    t_max = nh * nq * ((nb * KEEP + 1) // 2)
    t_max = -(-t_max // 128) * 128
    q_all, kv_all, work, turns = pl.pallas_call(
        functools.partial(project_exchange, nb, nh),
        out_shape=(
            jax.ShapeDtypeStruct((nh, nq // 2, BLK, BLK), BF16),
            jax.ShapeDtypeStruct((nb * KEEP, BLK, BLK), BF16),
            jax.ShapeDtypeStruct((8, t_max), jnp.int32),
            jax.ShapeDtypeStruct((8, 128), jnp.int32),
        ),
        in_specs=[smem, vmem, hbm, hbm, hbm, hbm],
        out_specs=(hbm, hbm, vmem, vmem),
        scratch_shapes=[
            pltpu.VMEM((nq, BLK, tokens.shape[1]), BF16),
            pltpu.VMEM(w_query.shape, BF16),
            pltpu.VMEM(w_key.shape, BF16),
            pltpu.VMEM(w_value.shape, BF16),
            pltpu.VMEM((nh, nq // 2, BLK, BLK), BF16),
            pltpu.VMEM((nh, KEEP, BLK, BLK), BF16),
            dma((nb,)),
            dma((nb,)),
            dma((nh,)),
            dma((nh,)),
            dma((2,)),
            dma((4,)),
        ],
        compiler_params=pltpu.CompilerParams(
            collective_id=0, has_side_effects=True, vmem_limit_bytes=32 * MIB
        ),
        name="project_exchange",
    )(block_mask, block_mask, tokens.reshape(nq, BLK, -1), w_query, w_key, w_value)
    att = pl.pallas_call(
        attend,
        out_shape=jax.ShapeDtypeStruct((nh * nq + 1, HD, BLK), BF16),
        in_specs=[smem, smem, vmem, vmem],
        out_specs=vmem,
        scratch_shapes=[
            pltpu.VMEM((nh * nq + 1, BLK, BLK), BF16),
            pltpu.VMEM((nb * KEEP, HD, BLK), BF16),
        ],
        compiler_params=pltpu.CompilerParams(vmem_limit_bytes=32 * MIB),
        name="attend",
    )(work, turns, q_all.reshape(nh * nq // 2, BLK, BLK), kv_all)
    n = nh * nz
    return pl.pallas_call(
        functools.partial(exchange_project, nh, nz),
        out_shape=jax.ShapeDtypeStruct((per * BLK, w_out.shape[1]), BF16),
        in_specs=[hbm, hbm],
        out_specs=vmem,
        scratch_shapes=[
            pltpu.VMEM((n, per, HD, BLK), BF16),
            pltpu.VMEM((w_out.shape[0] * nz, w_out.shape[1]), BF16),
            dma((n,)),
            dma((n,)),
            dma((2,)),
        ],
        compiler_params=pltpu.CompilerParams(
            collective_id=1, has_side_effects=True, vmem_limit_bytes=32 * MIB
        ),
        name="exchange_project",
    )(att, w_full)


def solution(mesh):
    return jax.shard_map(
        functools.partial(on_device, mesh.shape["band"], mesh.shape["head"]),
        mesh=mesh,
        in_specs=(
            P(("tiles", "band"), None),
            P(None, "head"),
            P(None, "head"),
            P(None, "head"),
            P("head", None),
            P("tiles", None),
        ),
        out_specs=P(("tiles", "band", "head"), None),
        check_vma=False,
    )
```

time: 97.3 us -> 82.8 us (0.85); the launches traced: 98.6 us -> 82.4 us
  Pallas kernels: 71.2 us -> 52 us
  waiting for transfers between devices: 0.73 us -> 9.16 us
  other arithmetic: 4.15 us -> 0 us
    pallas_call x1, Pallas kernels: 34.1 us -> 16.8 us  [on_device(): pl.pallas_call(attend, out_shape=jax.ShapeDtypeStruct((nh * nq + 1, HD, B...]
    all_gather x1, waiting for transfers between devices: 0.02 us -> 8.45 us  [on_device(): w_full = lax.all_gather(w_out, 'head', axis=0, tiled=True)]
    reduce_sum x7 -> x0, other arithmetic: 2.38 us -> none  [the longest x1 0.94 us: plan(): pos = jnp.sum(rows[:, :, None] * below[None], axis=1)]
    pallas_call x1, Pallas kernels: 17.1 us -> 15.6 us  [on_device(): pl.pallas_call(functools.partial(exchange_project, nh, nz), out_shape=jax...]
    unnamed x11 -> x13, local copies, waits for them, and re-layouts: 7.12 us -> 7.81 us
  transfers between devices with their start and end apart: 1 -> 1, of which waited for: 0 -> 1; matrix products, arithmetic and copies ran while one was open for 5% -> 0% of each run, Pallas kernels for 55% -> 44%
where the time goes in v2:
time: 82.8 us; the launch traced here: 82.4 us
  Pallas kernels  52 us (63%)
  between operations  13.4 us (16%)
  waiting for transfers between devices  9.16 us (11%)
  local copies, waits for them, and re-layouts  7.81 us (9%)
    pallas_call x1, Pallas kernels, on_device(): pl.pallas_call(functools.partial(project_exchange, nb, nh), out_shape=(ja...  19.6 us
    pallas_call x1, Pallas kernels, on_device(): pl.pallas_call(attend, out_shape=jax.ShapeDtypeStruct((nh * nq + 1, HD, B...  16.8 us
    pallas_call x1, Pallas kernels, on_device(): pl.pallas_call(functools.partial(exchange_project, nh, nz), out_shape=jax...  15.6 us
    all_gather x1, waiting for transfers between devices, on_device(): w_full = lax.all_gather(w_out, 'head', axis=0, tiled=True)  8.45 us
    unnamed x13, local copies, waits for them, and re-layouts  7.81 us
  transfers between devices with their start and end apart: 1, of which 1 were waited for; matrix products, arithmetic and copies ran while one was open for 0% of the time, Pallas kernels for 44%

profile of v2, /device:TPU:0, one launch (start us, length us, event | category | flops | bytes accessed | tf_op | source)
XLA Modules:
  0.0 82.4 jit_solution(10642894920747119481)
XLA Ops:
  6.5 0.0 all-gather.2.cloned.1.call-start
  6.5 0.7 all-gather.2.cloned.1.call-update
  7.3 0.0 copy-start
  7.3 1.6 %copy-done = bf16[1024,1024]{1,0:T(8,128)(2,1)S(1)} copy-done((bf16[1024,1024]{1,0:T(8,128)(2,1)S(1)}, bf16[1024,1024]{1,0:T(8,128)(2,1)}, u32[]{:S(2)}) %copy-start) | copy-done | bytes 2097176
  8.8 0.0 copy-start.2
  8.9 1.0 %copy-done.2 = bf16[1024,256]{1,0:T(8,128)(2,1)S(1)} copy-done((bf16[1024,256]{1,0:T(8,128)(2,1)S(1)}, bf16[1024,256]{1,0:T(8,128)(2,1)}, u32[]{:S(2)}) %copy-start.2) | copy-done | bytes 524312
  9.9 0.0 copy-start.3
  9.9 1.0 %copy-done.3 = bf16[1024,256]{1,0:T(8,128)(2,1)S(1)} copy-done((bf16[1024,256]{1,0:T(8,128)(2,1)S(1)}, bf16[1024,256]{1,0:T(8,128)(2,1)}, u32[]{:S(2)}) %copy-start.3) | copy-done | bytes 524312
  10.9 0.0 copy-start.4
  10.9 1.0 %copy-done.4 = bf16[1024,256]{1,0:T(8,128)(2,1)S(1)} copy-done((bf16[1024,256]{1,0:T(8,128)(2,1)S(1)}, bf16[1024,256]{1,0:T(8,128)(2,1)}, u32[]{:S(2)}) %copy-start.4) | copy-done | bytes 524312
  12.0 0.0 copy-start.5
  12.0 0.7 copy-done.5
  12.7 19.6 %project_exchange.1 = (bf16[4,4,128,128]{3,2,1,0:T(8,128)(2,1)S(1)}, bf16[24,128,128]{2,1,0:T(8,128)(2,1)S(1)}, s32[8,384]{1,0:T(8,128)S(1)}, s32[8,128]{1,0:T(8,128)S(1)}) custom-call(s32[32,32]{1,0:T(8,128)S(1)} %copy-done.5, s32[32,32]{1,0:T(8,128)S(1)} %copy-done.5, bf16[8,128,1024]{2,1,0:T(8,128)(2,1)S(1)} %bitcast.2, bf16[1024,256]{1,0:T(8,128)(2,1)S(1)} %copy-done.2, ...), custom_call_target="tpu_custom_call" | custom-call | tf_op jit(solution)/shard_map/project_exchange/pallas_call | solution.py:281
  32.3 16.8 %attend.1.att = bf16[33,64,128]{2,1,0:T(8,128)(2,1)S(1)} custom-call(s32[8,384]{1,0:T(8,128)S(1)} %get-tuple-element.9.work, s32[8,128]{1,0:T(8,128)S(1)} %get-tuple-element.10.turns, bf16[16,128,128]{2,1,0:T(8,128)(2,1)S(1)} %bitcast.3, bf16[24,128,128]{2,1,0:T(8,128)(2,1)S(1)} %get-tuple-element.12.kv), custom_call_target="tpu_custom_call" | custom-call | tf_op jit(solution)/shard_map/attend/pallas_call | solution.py:310
  49.2 8.4 %all-gather.2.cloned.1.call-done.w_hbm = bf16[1024,1024]{1,0:T(8,128)(2,1)} async-done(((bf16[256,1024]{1,0:T(8,128)(2,1)}), bf16[1024,1024]{1,0:T(8,128)(2,1)}) %all-gather.2.cloned.1.call-update) | async-done | bytes 2097168 | tf_op jit(solution)/shard_map/all_gather | solution.py:278
  57.6 0.0 copy-start.1
  57.6 1.6 %copy-done.1 = bf16[1024,1024]{1,0:T(8,128)(2,1)S(1)} copy-done((bf16[1024,1024]{1,0:T(8,128)(2,1)S(1)}, bf16[1024,1024]{1,0:T(8,128)(2,1)}, u32[]{:S(2)}) %copy-start.1) | copy-done | bytes 2097176
  59.2 15.6 %exchange_project.1 = bf16[256,1024]{1,0:T(8,128)(2,1)S(1)} custom-call(bf16[33,64,128]{2,1,0:T(8,128)(2,1)S(1)} %attend.1.att, bf16[1024,1024]{1,0:T(8,128)(2,1)S(1)} %copy-done.1), custom_call_target="tpu_custom_call" | custom-call | tf_op jit(solution)/shard_map/exchange_project/pallas_call | solution.py:323
  74.8 0.8 copy.8
Async XLA Ops:
  6.5 51.1 %all-gather.2.cloned.1.call-start = ((), (), s32[]{:S(2)}) async-start(), calls=%async_computation | async-start | bytes 2621440 | tf_op jit(solution)/shard_map/all_gather | solution.py:278
  7.3 1.6 %copy-start = (bf16[1024,1024]{1,0:T(8,128)(2,1)S(1)}, bf16[1024,1024]{1,0:T(8,128)(2,1)}, u32[]{:S(2)}) copy-start(bf16[1024,1024]{1,0:T(8,128)(2,1)} %param.6) | copy-start | bytes 6291460
  8.8 1.0 %copy-start.2 = (bf16[1024,256]{1,0:T(8,128)(2,1)S(1)}, bf16[1024,256]{1,0:T(8,128)(2,1)}, u32[]{:S(2)}) copy-start(bf16[1024,256]{1,0:T(8,128)(2,1)} %wq_hbm.1) | copy-start | bytes 1572868
  9.9 1.0 %copy-start.3 = (bf16[1024,256]{1,0:T(8,128)(2,1)S(1)}, bf16[1024,256]{1,0:T(8,128)(2,1)}, u32[]{:S(2)}) copy-start(bf16[1024,256]{1,0:T(8,128)(2,1)} %wk_hbm.1) | copy-start | bytes 1572868
  10.9 1.0 %copy-start.4 = (bf16[1024,256]{1,0:T(8,128)(2,1)S(1)}, bf16[1024,256]{1,0:T(8,128)(2,1)}, u32[]{:S(2)}) copy-start(bf16[1024,256]{1,0:T(8,128)(2,1)} %wv_hbm.1) | copy-start | bytes 1572868
  12.0 0.7 copy-start.5
  57.6 1.6 %copy-start.1 = (bf16[1024,1024]{1,0:T(8,128)(2,1)S(1)}, bf16[1024,1024]{1,0:T(8,128)(2,1)}, u32[]{:S(2)}) copy-start(bf16[1024,1024]{1,0:T(8,128)(2,1)} %all-gather.2.cloned.1.call-done.w_hbm) | copy-start | bytes 6291460
Sparse Core Ops, SparseCore 0:
  8.9 48.6 all-gather.1

commit v3 on v2

--- a/solution.py
+++ b/solution.py
@@ -9,7 +9,7 @@
 HD = 64
 BLK = 128
 KEEP = 6
-UNROLL = 4
+UNROLL = 8
 LOW = -1e30
 SCALE = HD**-0.5 * 1.4426950408889634
 MIB = 1 << 20

time: 82.8 us -> 82.8 us (level)
  waiting for transfers between devices: 9.16 us -> 14.6 us
  Pallas kernels: 52 us -> 46.6 us
    pallas_call x1, Pallas kernels: 16.8 us -> 11.4 us  [on_device(): pl.pallas_call(attend, out_shape=jax.ShapeDtypeStruct((nh * nq + 1, HD, B...]
    all_gather x1, waiting for transfers between devices: 8.45 us -> 13.9 us  [on_device(): w_full = lax.all_gather(w_out, 'head', axis=0, tiled=True)]
  transfers between devices with their start and end apart: 1 -> 1, of which waited for: 1 -> 1; matrix products, arithmetic and copies ran while one was open for 0% -> 0% of each run, Pallas kernels for 44% -> 38%
where the time goes in v3:
time: 82.8 us; the launch traced here: 82.4 us
  Pallas kernels  46.6 us (56%)
  waiting for transfers between devices  14.6 us (18%)
  between operations  13.4 us (16%)
  local copies, waits for them, and re-layouts  7.81 us (9%)
    pallas_call x1, Pallas kernels, on_device(): pl.pallas_call(functools.partial(project_exchange, nb, nh), out_shape=(ja...  19.6 us
    pallas_call x1, Pallas kernels, on_device(): pl.pallas_call(functools.partial(exchange_project, nh, nz), out_shape=jax...  15.6 us
    all_gather x1, waiting for transfers between devices, on_device(): w_full = lax.all_gather(w_out, 'head', axis=0, tiled=True)  13.9 us
    pallas_call x1, Pallas kernels, on_device(): pl.pallas_call(attend, out_shape=jax.ShapeDtypeStruct((nh * nq + 1, HD, B...  11.4 us
    unnamed x13, local copies, waits for them, and re-layouts  7.81 us
  transfers between devices with their start and end apart: 1, of which 1 were waited for; matrix products, arithmetic and copies ran while one was open for 0% of the time, Pallas kernels for 38%

profile of v3, /device:TPU:0, one launch (start us, length us, event | category | flops | bytes accessed | tf_op | source)
XLA Modules:
  0.0 82.4 jit_solution(6443806918551246883)
XLA Ops:
  6.5 0.0 all-gather.2.cloned.1.call-start
  6.5 0.7 all-gather.2.cloned.1.call-update
  7.3 0.0 copy-start
  7.3 1.6 %copy-done = bf16[1024,1024]{1,0:T(8,128)(2,1)S(1)} copy-done((bf16[1024,1024]{1,0:T(8,128)(2,1)S(1)}, bf16[1024,1024]{1,0:T(8,128)(2,1)}, u32[]{:S(2)}) %copy-start) | copy-done | bytes 2097176
  8.8 0.0 copy-start.2
  8.9 1.0 %copy-done.2 = bf16[1024,256]{1,0:T(8,128)(2,1)S(1)} copy-done((bf16[1024,256]{1,0:T(8,128)(2,1)S(1)}, bf16[1024,256]{1,0:T(8,128)(2,1)}, u32[]{:S(2)}) %copy-start.2) | copy-done | bytes 524312
  9.9 0.0 copy-start.3
  9.9 1.0 %copy-done.3 = bf16[1024,256]{1,0:T(8,128)(2,1)S(1)} copy-done((bf16[1024,256]{1,0:T(8,128)(2,1)S(1)}, bf16[1024,256]{1,0:T(8,128)(2,1)}, u32[]{:S(2)}) %copy-start.3) | copy-done | bytes 524312
  10.9 0.0 copy-start.4
  10.9 1.0 %copy-done.4 = bf16[1024,256]{1,0:T(8,128)(2,1)S(1)} copy-done((bf16[1024,256]{1,0:T(8,128)(2,1)S(1)}, bf16[1024,256]{1,0:T(8,128)(2,1)}, u32[]{:S(2)}) %copy-start.4) | copy-done | bytes 524312
  12.0 0.0 copy-start.5
  12.0 0.7 copy-done.5
  12.7 19.6 %project_exchange.1 = (bf16[4,4,128,128]{3,2,1,0:T(8,128)(2,1)S(1)}, bf16[24,128,128]{2,1,0:T(8,128)(2,1)S(1)}, s32[8,384]{1,0:T(8,128)S(1)}, s32[8,128]{1,0:T(8,128)S(1)}) custom-call(s32[32,32]{1,0:T(8,128)S(1)} %copy-done.5, s32[32,32]{1,0:T(8,128)S(1)} %copy-done.5, bf16[8,128,1024]{2,1,0:T(8,128)(2,1)S(1)} %bitcast.2, bf16[1024,256]{1,0:T(8,128)(2,1)S(1)} %copy-done.2, ...), custom_call_target="tpu_custom_call" | custom-call | tf_op jit(solution)/shard_map/project_exchange/pallas_call | solution.py:281
  32.3 11.4 %attend.1.att = bf16[33,64,128]{2,1,0:T(8,128)(2,1)S(1)} custom-call(s32[8,384]{1,0:T(8,128)S(1)} %get-tuple-element.9.work, s32[8,128]{1,0:T(8,128)S(1)} %get-tuple-element.10.turns, bf16[16,128,128]{2,1,0:T(8,128)(2,1)S(1)} %bitcast.3, bf16[24,128,128]{2,1,0:T(8,128)(2,1)S(1)} %get-tuple-element.12.kv), custom_call_target="tpu_custom_call" | custom-call | tf_op jit(solution)/shard_map/attend/pallas_call | solution.py:310
  43.7 13.9 %all-gather.2.cloned.1.call-done.w_hbm = bf16[1024,1024]{1,0:T(8,128)(2,1)} async-done(((bf16[256,1024]{1,0:T(8,128)(2,1)}), bf16[1024,1024]{1,0:T(8,128)(2,1)}) %all-gather.2.cloned.1.call-update) | async-done | bytes 2097168 | tf_op jit(solution)/shard_map/all_gather | solution.py:278
  57.6 0.0 copy-start.1
  57.6 1.6 %copy-done.1 = bf16[1024,1024]{1,0:T(8,128)(2,1)S(1)} copy-done((bf16[1024,1024]{1,0:T(8,128)(2,1)S(1)}, bf16[1024,1024]{1,0:T(8,128)(2,1)}, u32[]{:S(2)}) %copy-start.1) | copy-done | bytes 2097176
  59.2 15.6 %exchange_project.1 = bf16[256,1024]{1,0:T(8,128)(2,1)S(1)} custom-call(bf16[33,64,128]{2,1,0:T(8,128)(2,1)S(1)} %attend.1.att, bf16[1024,1024]{1,0:T(8,128)(2,1)S(1)} %copy-done.1), custom_call_target="tpu_custom_call" | custom-call | tf_op jit(solution)/shard_map/exchange_project/pallas_call | solution.py:323
  74.8 0.8 copy.8
Async XLA Ops:
  6.5 51.1 %all-gather.2.cloned.1.call-start = ((), (), s32[]{:S(2)}) async-start(), calls=%async_computation | async-start | bytes 2621440 | tf_op jit(solution)/shard_map/all_gather | solution.py:278
  7.3 1.6 %copy-start = (bf16[1024,1024]{1,0:T(8,128)(2,1)S(1)}, bf16[1024,1024]{1,0:T(8,128)(2,1)}, u32[]{:S(2)}) copy-start(bf16[1024,1024]{1,0:T(8,128)(2,1)} %param.6) | copy-start | bytes 6291460
  8.8 1.0 %copy-start.2 = (bf16[1024,256]{1,0:T(8,128)(2,1)S(1)}, bf16[1024,256]{1,0:T(8,128)(2,1)}, u32[]{:S(2)}) copy-start(bf16[1024,256]{1,0:T(8,128)(2,1)} %wq_hbm.1) | copy-start | bytes 1572868
  9.9 1.0 %copy-start.3 = (bf16[1024,256]{1,0:T(8,128)(2,1)S(1)}, bf16[1024,256]{1,0:T(8,128)(2,1)}, u32[]{:S(2)}) copy-start(bf16[1024,256]{1,0:T(8,128)(2,1)} %wk_hbm.1) | copy-start | bytes 1572868
  10.9 1.0 %copy-start.4 = (bf16[1024,256]{1,0:T(8,128)(2,1)S(1)}, bf16[1024,256]{1,0:T(8,128)(2,1)}, u32[]{:S(2)}) copy-start(bf16[1024,256]{1,0:T(8,128)(2,1)} %wv_hbm.1) | copy-start | bytes 1572868
  12.0 0.7 copy-start.5
  57.6 1.6 %copy-start.1 = (bf16[1024,1024]{1,0:T(8,128)(2,1)S(1)}, bf16[1024,1024]{1,0:T(8,128)(2,1)}, u32[]{:S(2)}) copy-start(bf16[1024,1024]{1,0:T(8,128)(2,1)} %all-gather.2.cloned.1.call-done.w_hbm) | copy-start | bytes 6291460
Sparse Core Ops, SparseCore 0:
  8.9 48.6 all-gather.1
